TPU v7x, 32 devices: a whole 2x2x4 slice. The times are simulated.
32 devices in a mesh: gx: 8 (over y, x, core), gy: 4 (over z).
Axes of the slice: x: 2, y: 2, z: 4, core: 2. Of those that a mesh axis runs over, the one named last changes fastest.
Arguments:
- fields: float32 [4, 3, 64, 8, 8, 128], P(None, None, None, 'gx', 'gy'), may hold values from -6 to 6
- velocity: float32 [2, 3, 64, 128, 8, 8], P(None, None, None, ('gx', 'gy')), may hold values from -3 to 3
Outputs:
- advanced: float32 [4, 3, 64, 8, 8, 128], P(None, None, None, 'gx', 'gy')
All inputs are finite; a program needn't handle non-finite values.
Results may differ from a plain program's by a relative error of at most 0.0003.
Values sent between devices are 32-bit elements; how exact they have to be, the bound alone decides.
A program may use at most 64 MiB of HBM per device.

v0:
```python
import functools

import jax
import jax.numpy as jnp
import numpy as np
from jax import lax
from jax.experimental import pallas as pl
from jax.experimental.pallas import tpu as pltpu
from jax.sharding import PartitionSpec as P

STEP_SIZE = 0.025
PENALTY = 3.0
MESH = pl.DeviceIdType.MESH


def derivative_table():
    points = np.array([-1.0, -1.0 / np.sqrt(5.0), 1.0 / np.sqrt(5.0), 1.0])
    weights_bary = np.ones(4)
    for first in range(4):
        for second in range(4):
            if first != second:
                weights_bary[first] = weights_bary[first] / (points[first] - points[second])
    table = np.zeros((4, 4))
    for first in range(4):
        for second in range(4):
            if first != second:
                table[first, second] = (
                    weights_bary[second] / weights_bary[first] / (points[first] - points[second])
                )
    return [[float(np.float32(table[p, q])) for q in range(4)] for p in range(4)]


TABLE = derivative_table()


def combine(p, parts):
    total = None
    for q in range(4):
        if q != p:
            term = TABLE[p][q] * parts[q]
            total = term if total is None else total + term
    return total


def d2(plane):
    parts = [plane[q : q + 1] for q in range(4)]
    return jnp.concatenate([combine(p, parts) for p in range(4)], axis=0)


def d3(plane):
    parts = [plane[:, q : q + 1] for q in range(4)]
    return jnp.concatenate([combine(p, parts) for p in range(4)], axis=1)


def load(ref, comp, a):
    return ref[comp, 128 * a : 128 * (a + 1), :].reshape(4, 4, 8, 128)


def store(ref, comp, a, value):
    ref[comp, 128 * a : 128 * (a + 1), :] = value.reshape(128, 128)


def turn(value, shift, axis):
    shape = value.shape
    rows = value.reshape(-1, 128)
    if axis == 1:
        return pltpu.roll(rows, shift, axis=1).reshape(shape)
    grouped = value.reshape(-1, 8, 128)
    return pltpu.roll(grouped, 4, axis=1).reshape(shape)


def kernel(
    count_x,
    count_y,
    fields_ref,
    speed_ref,
    out_ref,
    send_v,
    recv_v,
    layers,
    speeds,
    state,
    middle,
    half,
    elec,
    send_x,
    recv_x,
    send_y,
    recv_y,
    sem_vs,
    sem_vr,
    sem_xs,
    sem_xr,
    sem_ys,
    sem_yr,
):
    gx = lax.axis_index("gx")
    gy = lax.axis_index("gy")
    devices = count_x * count_y
    me = gx * count_y + gy
    krylov = fields_ref.shape[0]
    phases, _, slab, wide_x, wide_y, _ = speed_ref.shape

    barrier = pltpu.get_barrier_semaphore()

    def partner(i):
        other = lax.rem(me + i, devices)
        return other, (lax.div(other, count_y), lax.rem(other, count_y))

    def greet(i, carry):
        _, where = partner(i)
        pl.semaphore_signal(barrier, inc=1, device_id=where, device_id_type=MESH)
        return carry

    lax.fori_loop(1, devices, greet, 0)

    lane8 = lax.broadcasted_iota(jnp.int32, (wide_y, 128), 1)

    def pack_phase(s):
        def pack(x, carry):
            for c in range(3):
                for z in range(slab):
                    tile = speed_ref[s, c, z, x]
                    wide = jnp.concatenate([tile, tile], axis=1)
                    wide = jnp.where(lane8 < 64, wide, pltpu.roll(wide, wide_y - 1, axis=0))
                    for g in range(count_y):
                        send_v[s, x * count_y + g, c, z : z + 1, :] = wide[2 * g : 2 * g + 1]
            return carry

        lax.fori_loop(0, count_x, pack, 0)

    def speed_copy(s, other, where):
        return pltpu.make_async_remote_copy(
            src_ref=send_v.at[s, other],
            dst_ref=recv_v.at[s, me],
            send_sem=sem_vs.at[s, other],
            recv_sem=sem_vr.at[s, me],
            device_id=where,
            device_id_type=MESH,
        )

    def send_phase(s):
        def send(i, carry):
            other, where = partner(i)
            speed_copy(s, other, where).start()
            return carry

        lax.fori_loop(1, devices, send, 0)
        pltpu.make_async_copy(send_v.at[s, me], recv_v.at[s, me], sem_vr.at[s, me]).start()

    def finish_phase(s):
        def take(src, carry):
            pltpu.make_async_copy(recv_v.at[s, src], recv_v.at[s, src], sem_vr.at[s, src]).wait()
            return carry

        lax.fori_loop(0, devices, take, 0)
        for c in range(3):
            for src in range(devices):
                layers[c, slab * src : slab * (src + 1), :] = recv_v[s, src, c]
            turned = layers[c].T
            for y in range(2):
                for i in range(8):
                    rows = turned[64 * y + 8 * i : 64 * y + 8 * (i + 1)]
                    for k in range(4):
                        speeds[s, c, pl.ds(64 * i + 4 * y + k, 8, stride=8), :] = rows

    def drain_phase(s):
        def drain(i, carry):
            other, where = partner(i)
            speed_copy(s, other, where).wait_send()
            return carry

        lax.fori_loop(1, devices, drain, 0)

    has_low_x = gx > 0
    has_high_x = gx < count_x - 1
    has_low_y = gy > 0
    has_high_y = gy < count_y - 1

    def halo_copy(stage, axis, side):
        step = 1 if side == 0 else -1
        if axis == 0:
            where = (gx + step, gy)
            src, dst, ss, sr = send_x, recv_x, sem_xs, sem_xr
        else:
            where = (gx, gy + step)
            src, dst, ss, sr = send_y, recv_y, sem_ys, sem_yr
        return pltpu.make_async_remote_copy(
            src_ref=src.at[stage, side],
            dst_ref=dst.at[stage, side],
            send_sem=ss.at[stage, side],
            recv_sem=sr.at[stage, side],
            device_id=where,
            device_id_type=MESH,
        )

    halos = [
        (0, 0, has_high_x, has_low_x),
        (0, 1, has_low_x, has_high_x),
        (1, 0, has_high_y, has_low_y),
        (1, 1, has_low_y, has_high_y),
    ]

    def halo_start(stage, axis):
        for which, side, sends, _ in halos:
            if which == axis:

                @pl.when(sends)
                def _():
                    halo_copy(stage, axis, side).start()

    def halo_wait(stage, axis):
        for which, side, _, takes in halos:
            if which == axis:

                @pl.when(takes)
                def _():
                    halo_copy(stage, axis, side).wait_recv()

    def halo_drain(stage):
        for which, side, sends, _ in halos:

            @pl.when(sends)
            def _():
                halo_copy(stage, which, side).wait_send()

    row = lax.broadcasted_iota(jnp.int32, (1, 1, 8, 128), 2)
    lane = lax.broadcasted_iota(jnp.int32, (1, 1, 8, 128), 3)

    def cross_plane(field, s, a):
        b = [load(field, c, a) for c in range(3)]
        u = [load(speeds.at[s], c, a) for c in range(3)]
        e = [u[1] * b[2] - u[2] * b[1], u[2] * b[0] - u[0] * b[2], u[0] * b[1] - u[1] * b[0]]
        for c in range(3):
            store(elec, c, a, e[c])
        return b, e

    def begin(field, s, stage):
        b, e = cross_plane(field, s, 0)
        low = [b[0], b[1] - e[2], b[2] + e[1]]
        for c in range(3):
            send_x[stage, 1, c] = low[c].reshape(128, 128)
        b, e = cross_plane(field, s, 3)
        high = [b[0], b[1] + e[2], b[2] - e[1]]
        for c in range(3):
            send_x[stage, 0, c] = high[c].reshape(128, 128)
        halo_start(stage, 0)
        for a in (1, 2):
            cross_plane(field, s, a)
        for a in range(4):
            b = [load(field, c, a) for c in range(3)]
            e = [load(elec, c, a) for c in range(3)]
            low = [b[0][0:1] + e[2][0:1], b[1][0:1], b[2][0:1] - e[0][0:1]]
            high = [b[0][3:4] - e[2][3:4], b[1][3:4], b[2][3:4] + e[0][3:4]]
            for c in range(3):
                first = jnp.where(row < 4, low[c][:, 0:2], turn(low[c][:, 2:4], 4, 0))
                second = jnp.where(row < 4, turn(high[c][:, 0:2], 4, 0), high[c][:, 2:4])
                send_y[stage, 1, c, 16 * a : 16 * (a + 1), :] = first.reshape(16, 128)
                send_y[stage, 0, c, 16 * a : 16 * (a + 1), :] = second.reshape(16, 128)
        halo_start(stage, 1)

    def volume(field, a):
        b = [load(field, c, a) for c in range(3)]
        e = [load(elec, c, a) for c in range(3)]
        r = [
            d2(e[2]) - d3(e[1]),
            d3(e[0]) - combine(a, [load(elec, 2, q) for q in range(4)]),
            combine(a, [load(elec, 1, q) for q in range(4)]) - d2(e[0]),
        ]
        low2 = [b[0] - e[1], b[1] + e[0], b[2]]
        high2 = [b[0] + e[1], b[1] - e[0], b[2]]
        low1 = [b[0] + e[2], b[1], b[2] - e[0]]
        high1 = [b[0] - e[2], b[1], b[2] + e[0]]
        for c in range(3):
            from_below = jnp.where(lane > 0, turn(high2[c][:, 3:4], 1, 1), 0.0)
            from_above = jnp.where(lane < 127, turn(low2[c][:, 0:1], 127, 1), 0.0)
            gap = jnp.zeros((4, 2, 8, 128), jnp.float32)
            jump = jnp.concatenate(
                [from_below - b[c][:, 0:1], gap, from_above - b[c][:, 3:4]], axis=1
            )
            from_below = jnp.where(row >= 4, turn(high1[c][3:4], 4, 0), 0.0)
            from_above = jnp.where(row < 4, turn(low1[c][0:1], 4, 0), 0.0)
            gap = jnp.zeros((2, 4, 8, 128), jnp.float32)
            jump = jump + jnp.concatenate(
                [from_below - b[c][0:1], gap, from_above - b[c][3:4]], axis=0
            )
            if a in (0, 3):
                jump = jump - b[c]
            r[c] = r[c] + PENALTY * jump
        return b, r

    def add_halo(stage, targets):
        halo_wait(stage, 0)
        for c in range(3):
            for side, a in ((0, 0), (1, 3)):
                arrived = recv_x[stage, side, c].reshape(4, 4, 8, 128)
                for ref, scale in targets:
                    store(ref, c, a, load(ref, c, a) + (scale * PENALTY) * arrived)
        halo_wait(stage, 1)
        for c in range(3):
            for a in range(4):
                for side, b in ((0, 0), (1, 3)):
                    got = recv_y[stage, side, c, 16 * a : 16 * (a + 1), :].reshape(1, 2, 8, 128)
                    back = turn(got, 4, 0)
                    if side == 0:
                        arrived = jnp.concatenate([got, back], axis=1)
                        arrived = jnp.where(row < 4, arrived, 0.0)
                    else:
                        arrived = jnp.concatenate([back, got], axis=1)
                        arrived = jnp.where(row >= 4, arrived, 0.0)
                    at = 128 * a + 32 * b
                    arrived = arrived.reshape(32, 128)
                    for ref, scale in targets:
                        ref[c, at : at + 32, :] = (
                            ref[c, at : at + 32, :] + (scale * PENALTY) * arrived
                        )

    for which, side, _, takes in halos:

        @pl.when(jnp.logical_not(takes))
        def _():
            buffer = recv_x if which == 0 else recv_y
            for stage in range(2 * phases):
                for c in range(3):
                    buffer[stage, side, c] = jnp.zeros(buffer.shape[3:], jnp.float32)

    pack_phase(0)
    pl.semaphore_wait(barrier, devices - 1)
    send_phase(0)
    for s in range(1, phases):
        pack_phase(s)

    for k in range(krylov):
        for c in range(3):
            for j in range(16):
                state[c, pl.ds(32 * j + k, 8, stride=4), :] = fields_ref[
                    k, c, 8 * j : 8 * (j + 1), :
                ]

    for s in range(phases):
        finish_phase(s)
        stage = 2 * s
        begin(state, s, stage)
        if s + 1 < phases:
            send_phase(s + 1)
        for a in range(4):
            b, r = volume(state, a)
            for c in range(3):
                store(middle, c, a, b[c] + STEP_SIZE * r[c])
                store(half, c, a, b[c] + (0.5 * STEP_SIZE) * r[c])
        add_halo(stage, [(middle, STEP_SIZE), (half, 0.5 * STEP_SIZE)])
        begin(middle, s, stage + 1)
        for a in range(4):
            _, r = volume(middle, a)
            for c in range(3):
                store(state, c, a, load(half, c, a) + (0.5 * STEP_SIZE) * r[c])
        add_halo(stage + 1, [(state, 0.5 * STEP_SIZE)])

    for k in range(krylov):
        for c in range(3):
            for j in range(16):
                out_ref[k, c, 8 * j : 8 * (j + 1), :] = state[
                    c, pl.ds(32 * j + k, 8, stride=4), :
                ]

    for s in range(phases):
        drain_phase(s)
    for stage in range(2 * phases):
        halo_drain(stage)


def shards(count_x, count_y, fields, velocity):
    krylov, comps, nodes, elem_x, elem_y, depth = fields.shape
    phases, _, _, slab, wide_x, wide_y = velocity.shape
    devices = count_x * count_y
    stages = 2 * phases
    f32 = jnp.float32
    rows = nodes * elem_x * elem_y
    lines = krylov * rows
    body = functools.partial(kernel, count_x, count_y)
    vmem = pl.BlockSpec(memory_space=pltpu.VMEM)
    out = pl.pallas_call(
        body,
        out_shape=jax.ShapeDtypeStruct((krylov, comps, rows, depth), f32),
        in_specs=[vmem, vmem],
        out_specs=vmem,
        scratch_shapes=[
            pltpu.VMEM((phases, devices, comps, slab, 128), f32),
            pltpu.VMEM((phases, devices, comps, slab, 128), f32),
            pltpu.VMEM((comps, depth, 128), f32),
            pltpu.VMEM((phases, comps, lines, depth), f32),
            pltpu.VMEM((comps, lines, depth), f32),
            pltpu.VMEM((comps, lines, depth), f32),
            pltpu.VMEM((comps, lines, depth), f32),
            pltpu.VMEM((comps, lines, depth), f32),
            pltpu.VMEM((stages, 2, comps, 128, depth), f32),
            pltpu.VMEM((stages, 2, comps, 128, depth), f32),
            pltpu.VMEM((stages, 2, comps, 64, depth), f32),
            pltpu.VMEM((stages, 2, comps, 64, depth), f32),
            pltpu.SemaphoreType.DMA((phases, devices)),
            pltpu.SemaphoreType.DMA((phases, devices)),
            pltpu.SemaphoreType.DMA((stages, 2)),
            pltpu.SemaphoreType.DMA((stages, 2)),
            pltpu.SemaphoreType.DMA((stages, 2)),
            pltpu.SemaphoreType.DMA((stages, 2)),
        ],
        compiler_params=pltpu.CompilerParams(
            collective_id=0, has_side_effects=True, vmem_limit_bytes=48 * 1024 * 1024
        ),
    )(
        fields.reshape(krylov, comps, rows, depth),
        jnp.transpose(velocity, (0, 1, 3, 4, 5, 2)),
    )
    return out.reshape(fields.shape)


def solution(mesh):
    return jax.shard_map(
        functools.partial(shards, mesh.shape["gx"], mesh.shape["gy"]),
        mesh=mesh,
        in_specs=(
            P(None, None, None, "gx", "gy", None),
            P(None, None, None, ("gx", "gy"), None, None),
        ),
        out_specs=P(None, None, None, "gx", "gy", None),
        check_vma=False,
    )
```

profile of v0, /device:TPU:3, one launch (start us, length us, event | category | flops | bytes accessed | tf_op | source)
XLA Modules:
  0.0 41.0 jit_solution(6784727249637423492)
XLA Ops:
  0.0 0.0 copy-start
  0.0 1.1 %copy-done = f32[4,3,64,1,2,128]{5,4,3,2,1,0:T(2,128)S(1)} copy-done((f32[4,3,64,1,2,128]{5,4,3,2,1,0:T(2,128)S(1)}, f32[4,3,64,1,2,128]{5,4,3,2,1,0:T(2,128)}, u32[]{:S(2)}) %copy-start) | copy-done | bytes 786456
  1.1 0.0 copy-start.1
  1.1 1.1 %copy-done.1 = f32[2,3,64,4,8,8]{2,5,4,3,1,0:T(8,128)S(1)} copy-done((f32[2,3,64,4,8,8]{2,5,4,3,1,0:T(8,128)S(1)}, f32[2,3,64,4,8,8]{2,5,4,3,1,0:T(8,128)}, u32[]{:S(2)}) %copy-start.1) | copy-done | bytes 393240
  2.3 37.9 %shard_map.28 = f32[4,3,128,128]{3,2,1,0:T(8,128)S(1)} custom-call(f32[4,3,128,128]{3,2,1,0:T(8,128)S(1)} %bitcast.6, f32[2,3,4,8,8,64]{5,4,3,2,1,0:T(8,128)S(1)} %bitcast.7), custom_call_target="tpu_custom_call" | custom-call | tf_op jit(solution)/shard_map/pallas_call | solution.py:382
  40.1 0.9 %copy.5 = f32[4,3,64,1,2,128]{5,4,3,2,1,0:T(2,128)} copy(f32[4,3,64,1,2,128]{5,4,3,2,1,0:T(2,128)S(1)} %bitcast.5) | data formatting | bytes 1572864
Async XLA Ops:
  0.0 1.1 %copy-start = (f32[4,3,64,1,2,128]{5,4,3,2,1,0:T(2,128)S(1)}, f32[4,3,64,1,2,128]{5,4,3,2,1,0:T(2,128)}, u32[]{:S(2)}) copy-start(f32[4,3,64,1,2,128]{5,4,3,2,1,0:T(2,128)} %param.2) | copy-start | bytes 2359300
  1.1 1.1 %copy-start.1 = (f32[2,3,64,4,8,8]{2,5,4,3,1,0:T(8,128)S(1)}, f32[2,3,64,4,8,8]{2,5,4,3,1,0:T(8,128)}, u32[]{:S(2)}) copy-start(f32[2,3,64,4,8,8]{2,5,4,3,1,0:T(8,128)} %param.3) | copy-start | bytes 1179652
where the time goes:
time: 41.2 us; the launch traced here: 41 us
  Pallas kernels  37.9 us (92%)
  local copies, waits for them, and re-layouts  3.15 us (8%)
    pallas_call x1, Pallas kernels, shards(): pl.pallas_call(body, out_shape=jax.ShapeDtypeStruct((krylov, comps, rows,...  37.9 us
    unnamed x5, local copies, waits for them, and re-layouts  3.15 us

commit v1 on v0

--- a/solution.py
+++ b/solution.py
@@ -72,9 +72,11 @@
 def kernel(
     count_x,
     count_y,
+    fields_any,
+    speed_any,
+    out_ref,
     fields_ref,
     speed_ref,
-    out_ref,
     send_v,
     recv_v,
     layers,
@@ -93,6 +95,7 @@
     sem_xr,
     sem_ys,
     sem_yr,
+    sem_in,
 ):
     gx = lax.axis_index("gx")
     gy = lax.axis_index("gy")
@@ -100,6 +103,14 @@
     me = gx * count_y + gy
     krylov = fields_ref.shape[0]
     phases, _, slab, wide_x, wide_y, _ = speed_ref.shape
+
+    loads = [
+        pltpu.make_async_copy(speed_any.at[s], speed_ref.at[s], sem_in.at[s])
+        for s in range(phases)
+    ]
+    loads.append(pltpu.make_async_copy(fields_any, fields_ref, sem_in.at[phases]))
+    for item in loads:
+        item.start()
 
     barrier = pltpu.get_barrier_semaphore()
 
@@ -201,9 +212,9 @@
         (1, 1, has_low_y, has_high_y),
     ]
 
-    def halo_start(stage, axis):
+    def halo_start(stage, axis, sides=(0, 1)):
         for which, side, sends, _ in halos:
-            if which == axis:
+            if which == axis and side in sides:
 
                 @pl.when(sends)
                 def _():
@@ -240,11 +251,12 @@
         low = [b[0], b[1] - e[2], b[2] + e[1]]
         for c in range(3):
             send_x[stage, 1, c] = low[c].reshape(128, 128)
+        halo_start(stage, 0, (1,))
         b, e = cross_plane(field, s, 3)
         high = [b[0], b[1] + e[2], b[2] - e[1]]
         for c in range(3):
             send_x[stage, 0, c] = high[c].reshape(128, 128)
-        halo_start(stage, 0)
+        halo_start(stage, 0, (0,))
         for a in (1, 2):
             cross_plane(field, s, a)
         for a in range(4):
@@ -324,11 +336,14 @@
                 for c in range(3):
                     buffer[stage, side, c] = jnp.zeros(buffer.shape[3:], jnp.float32)
 
+    loads[0].wait()
     pack_phase(0)
     pl.semaphore_wait(barrier, devices - 1)
     send_phase(0)
     for s in range(1, phases):
+        loads[s].wait()
         pack_phase(s)
+    loads[phases].wait()
 
     for k in range(krylov):
         for c in range(3):
@@ -337,8 +352,8 @@
                     k, c, 8 * j : 8 * (j + 1), :
                 ]
 
+    finish_phase(0)
     for s in range(phases):
-        finish_phase(s)
         stage = 2 * s
         begin(state, s, stage)
         if s + 1 < phases:
@@ -354,6 +369,8 @@
             _, r = volume(middle, a)
             for c in range(3):
                 store(state, c, a, load(half, c, a) + (0.5 * STEP_SIZE) * r[c])
+        if s + 1 < phases:
+            finish_phase(s + 1)
         add_halo(stage + 1, [(state, 0.5 * STEP_SIZE)])
 
     for k in range(krylov):
@@ -382,9 +399,11 @@
     out = pl.pallas_call(
         body,
         out_shape=jax.ShapeDtypeStruct((krylov, comps, rows, depth), f32),
-        in_specs=[vmem, vmem],
+        in_specs=[pl.BlockSpec(memory_space=pl.ANY)] * 2,
         out_specs=vmem,
         scratch_shapes=[
+            pltpu.VMEM((krylov, comps, rows, depth), f32),
+            pltpu.VMEM((phases, comps, slab, wide_x, wide_y, nodes), f32),
             pltpu.VMEM((phases, devices, comps, slab, 128), f32),
             pltpu.VMEM((phases, devices, comps, slab, 128), f32),
             pltpu.VMEM((comps, depth, 128), f32),
@@ -403,9 +422,10 @@
             pltpu.SemaphoreType.DMA((stages, 2)),
             pltpu.SemaphoreType.DMA((stages, 2)),
             pltpu.SemaphoreType.DMA((stages, 2)),
+            pltpu.SemaphoreType.DMA((phases + 1,)),
         ],
         compiler_params=pltpu.CompilerParams(
-            collective_id=0, has_side_effects=True, vmem_limit_bytes=48 * 1024 * 1024
+            collective_id=0, has_side_effects=True, vmem_limit_bytes=59392 * 1024
         ),
     )(
         fields.reshape(krylov, comps, rows, depth),

time: 41.2 us -> 40.8 us (level)
  local copies, waits for them, and re-layouts: 3.15 us -> 2.06 us
  Pallas kernels: 37.9 us -> 38.6 us
    unnamed x5 -> x1, local copies, waits for them, and re-layouts: 3.15 us -> 2.06 us
    pallas_call x1, Pallas kernels: 37.9 us -> 38.6 us  [shards(): pl.pallas_call(body, out_shape=jax.ShapeDtypeStruct((krylov, comps, rows,...]
where the time goes in v1:
time: 40.8 us; the launch traced here: 40.6 us
  Pallas kernels  38.6 us (95%)
  local copies, waits for them, and re-layouts  2.06 us (5%)
    pallas_call x1, Pallas kernels, shards(): pl.pallas_call(body, out_shape=jax.ShapeDtypeStruct((krylov, comps, rows,...  38.6 us
    unnamed x1, local copies, waits for them, and re-layouts  2.06 us

profile of v1, /device:TPU:3, one launch (start us, length us, event | category | flops | bytes accessed | tf_op | source)
XLA Modules:
  0.0 40.6 jit_solution(15394651573886217774)
XLA Ops:
  0.0 38.6 %shard_map.28 = f32[4,3,128,128]{3,2,1,0:T(8,128)} custom-call(f32[4,3,128,128]{3,2,1,0:T(8,128)} %bitcast.6, f32[2,3,4,8,8,64]{5,4,3,2,1,0:T(8,128)} %bitcast.7), custom_call_target="tpu_custom_call" | custom-call | tf_op jit(solution)/shard_map/pallas_call | solution.py:399
  38.6 2.1 %copy.5 = f32[4,3,64,1,2,128]{5,4,3,2,1,0:T(2,128)} copy(f32[4,3,64,1,2,128]{5,4,3,2,1,0:T(2,128)} %bitcast.5) | data formatting | bytes 1572864

commit v2 on v1

--- a/solution.py
+++ b/solution.py
@@ -83,7 +83,6 @@
     speeds,
     state,
     middle,
-    half,
     elec,
     send_x,
     recv_x,
@@ -188,7 +187,7 @@
     has_low_y = gy > 0
     has_high_y = gy < count_y - 1
 
-    def halo_copy(stage, axis, side):
+    def halo_copy(stage, axis, side, part):
         step = 1 if side == 0 else -1
         if axis == 0:
             where = (gx + step, gy)
@@ -197,79 +196,151 @@
             where = (gx, gy + step)
             src, dst, ss, sr = send_y, recv_y, sem_ys, sem_yr
         return pltpu.make_async_remote_copy(
-            src_ref=src.at[stage, side],
-            dst_ref=dst.at[stage, side],
-            send_sem=ss.at[stage, side],
-            recv_sem=sr.at[stage, side],
+            src_ref=src.at[stage, side, part],
+            dst_ref=dst.at[stage, side, part],
+            send_sem=ss.at[stage, side, part],
+            recv_sem=sr.at[stage, side, part],
             device_id=where,
             device_id_type=MESH,
         )
 
-    halos = [
-        (0, 0, has_high_x, has_low_x),
-        (0, 1, has_low_x, has_high_x),
-        (1, 0, has_high_y, has_low_y),
-        (1, 1, has_low_y, has_high_y),
-    ]
-
-    def halo_start(stage, axis, sides=(0, 1)):
-        for which, side, sends, _ in halos:
-            if which == axis and side in sides:
-
-                @pl.when(sends)
+    sends = [[has_high_x, has_low_x], [has_high_y, has_low_y]]
+    takes = [[has_low_x, has_high_x], [has_low_y, has_high_y]]
+
+    def halo_start(stage, axis, side, part):
+        @pl.when(sends[axis][side])
+        def _():
+            halo_copy(stage, axis, side, part).start()
+
+    def halo_wait(stage, axis, side, part):
+        @pl.when(takes[axis][side])
+        def _():
+            halo_copy(stage, axis, side, part).wait_recv()
+
+    def halo_drain(stage):
+        for axis in range(2):
+            for side in range(2):
+
+                @pl.when(sends[axis][side])
                 def _():
-                    halo_copy(stage, axis, side).start()
-
-    def halo_wait(stage, axis):
-        for which, side, _, takes in halos:
-            if which == axis:
-
-                @pl.when(takes)
-                def _():
-                    halo_copy(stage, axis, side).wait_recv()
-
-    def halo_drain(stage):
-        for which, side, sends, _ in halos:
-
-            @pl.when(sends)
-            def _():
-                halo_copy(stage, which, side).wait_send()
+                    for part in range(2):
+                        halo_copy(stage, axis, side, part).wait_send()
 
     row = lax.broadcasted_iota(jnp.int32, (1, 1, 8, 128), 2)
     lane = lax.broadcasted_iota(jnp.int32, (1, 1, 8, 128), 3)
 
-    def cross_plane(field, s, a):
-        b = [load(field, c, a) for c in range(3)]
-        u = [load(speeds.at[s], c, a) for c in range(3)]
-        e = [u[1] * b[2] - u[2] * b[1], u[2] * b[0] - u[0] * b[2], u[0] * b[1] - u[1] * b[0]]
-        for c in range(3):
-            store(elec, c, a, e[c])
-        return b, e
-
-    def begin(field, s, stage):
-        b, e = cross_plane(field, s, 0)
-        low = [b[0], b[1] - e[2], b[2] + e[1]]
-        for c in range(3):
-            send_x[stage, 1, c] = low[c].reshape(128, 128)
-        halo_start(stage, 0, (1,))
-        b, e = cross_plane(field, s, 3)
-        high = [b[0], b[1] + e[2], b[2] - e[1]]
-        for c in range(3):
-            send_x[stage, 0, c] = high[c].reshape(128, 128)
-        halo_start(stage, 0, (0,))
+    row3 = lax.broadcasted_iota(jnp.int32, (1, 8, 128), 1)
+
+    def block(a, b):
+        return slice(128 * a + 32 * b, 128 * a + 32 * (b + 1))
+
+    def cross_block(field, s, a, b):
+        at = block(a, b)
+        f = [field[c, at, :].reshape(4, 8, 128) for c in range(3)]
+        u = [speeds[s, c, at, :].reshape(4, 8, 128) for c in range(3)]
+        e = [u[1] * f[2] - u[2] * f[1], u[2] * f[0] - u[0] * f[2], u[0] * f[1] - u[1] * f[0]]
+        for c in range(3):
+            elec[c, at, :] = e[c].reshape(32, 128)
+        return f, e
+
+    def pack_x(stage, a, b, f, e):
+        if a == 0:
+            face = [f[0], f[1] - e[2], f[2] + e[1]]
+        else:
+            face = [f[0], f[1] + e[2], f[2] - e[1]]
+        part, slot = (0, b - 1) if b in (1, 2) else (1, b // 3)
+        for c in range(3):
+            send_x[stage, 1 - a // 3, part, c, 32 * slot : 32 * (slot + 1), :] = face[c].reshape(
+                32, 128
+            )
+
+    def pack_y(stage, a, b, f, e):
+        if b == 0:
+            face = [f[0] + e[2], f[1], f[2] - e[0]]
+        else:
+            face = [f[0] - e[2], f[1], f[2] + e[0]]
+        part, slot = (0, a - 1) if a in (1, 2) else (1, a // 3)
+        for c in range(3):
+            if b == 0:
+                both = jnp.where(row3 < 4, face[c][0:2], turn(face[c][2:4], 4, 0))
+            else:
+                both = jnp.where(row3 < 4, turn(face[c][0:2], 4, 0), face[c][2:4])
+            send_y[stage, 1 - b // 3, part, c, 16 * slot : 16 * (slot + 1), :] = both.reshape(
+                16, 128
+            )
+
+    def arrived_x(stage, a, b):
+        part, slot = (0, b - 1) if b in (1, 2) else (1, b // 3)
+        return [
+            recv_x[stage, a // 3, part, c, 32 * slot : 32 * (slot + 1), :] for c in range(3)
+        ]
+
+    def arrived_y(stage, a, b):
+        part, slot = (0, a - 1) if a in (1, 2) else (1, a // 3)
+        found = []
+        for c in range(3):
+            got = recv_y[stage, b // 3, part, c, 16 * slot : 16 * (slot + 1), :]
+            got = got.reshape(2, 8, 128)
+            back = turn(got, 4, 0)
+            if b == 0:
+                full = jnp.where(row3 < 4, jnp.concatenate([got, back], axis=0), 0.0)
+            else:
+                full = jnp.where(row3 >= 4, jnp.concatenate([back, got], axis=0), 0.0)
+            found.append(full.reshape(32, 128))
+        return found
+
+    def add_block(target, a, b, found, scale):
+        at = block(a, b)
+        for c in range(3):
+            target[c, at, :] = target[c, at, :] + (scale * PENALTY) * found[c]
+
+    def rims(target, s, stage, scale, arrive, onward):
+        for a in (0, 3):
+            if arrive:
+                halo_wait(stage, 0, a // 3, 0)
+            for b in (1, 2):
+                if arrive:
+                    add_block(target, a, b, arrived_x(stage, a, b), scale)
+                if onward:
+                    f, e = cross_block(target, s, a, b)
+                    pack_x(stage + 1, a, b, f, e)
+            if onward:
+                halo_start(stage + 1, 0, 1 - a // 3, 0)
+        for b in (0, 3):
+            if arrive:
+                halo_wait(stage, 1, b // 3, 0)
+            for a in (1, 2):
+                if arrive:
+                    add_block(target, a, b, arrived_y(stage, a, b), scale)
+                if onward:
+                    f, e = cross_block(target, s, a, b)
+                    pack_y(stage + 1, a, b, f, e)
+            if onward:
+                halo_start(stage + 1, 1, 1 - b // 3, 0)
+        if arrive:
+            for axis in range(2):
+                for side in range(2):
+                    halo_wait(stage, axis, side, 1)
+        for a in (0, 3):
+            for b in (0, 3):
+                if arrive:
+                    fx = arrived_x(stage, a, b)
+                    fy = arrived_y(stage, a, b)
+                    add_block(target, a, b, [fx[c] + fy[c] for c in range(3)], scale)
+                if onward:
+                    f, e = cross_block(target, s, a, b)
+                    pack_x(stage + 1, a, b, f, e)
+                    pack_y(stage + 1, a, b, f, e)
+            if onward:
+                halo_start(stage + 1, 0, 1 - a // 3, 1)
+        if onward:
+            for side in range(2):
+                halo_start(stage + 1, 1, side, 1)
+
+    def inner(field, s):
         for a in (1, 2):
-            cross_plane(field, s, a)
-        for a in range(4):
-            b = [load(field, c, a) for c in range(3)]
-            e = [load(elec, c, a) for c in range(3)]
-            low = [b[0][0:1] + e[2][0:1], b[1][0:1], b[2][0:1] - e[0][0:1]]
-            high = [b[0][3:4] - e[2][3:4], b[1][3:4], b[2][3:4] + e[0][3:4]]
-            for c in range(3):
-                first = jnp.where(row < 4, low[c][:, 0:2], turn(low[c][:, 2:4], 4, 0))
-                second = jnp.where(row < 4, turn(high[c][:, 0:2], 4, 0), high[c][:, 2:4])
-                send_y[stage, 1, c, 16 * a : 16 * (a + 1), :] = first.reshape(16, 128)
-                send_y[stage, 0, c, 16 * a : 16 * (a + 1), :] = second.reshape(16, 128)
-        halo_start(stage, 1)
+            for b in (1, 2):
+                cross_block(field, s, a, b)
 
     def volume(field, a):
         b = [load(field, c, a) for c in range(3)]
@@ -301,40 +372,15 @@
             r[c] = r[c] + PENALTY * jump
         return b, r
 
-    def add_halo(stage, targets):
-        halo_wait(stage, 0)
-        for c in range(3):
-            for side, a in ((0, 0), (1, 3)):
-                arrived = recv_x[stage, side, c].reshape(4, 4, 8, 128)
-                for ref, scale in targets:
-                    store(ref, c, a, load(ref, c, a) + (scale * PENALTY) * arrived)
-        halo_wait(stage, 1)
-        for c in range(3):
-            for a in range(4):
-                for side, b in ((0, 0), (1, 3)):
-                    got = recv_y[stage, side, c, 16 * a : 16 * (a + 1), :].reshape(1, 2, 8, 128)
-                    back = turn(got, 4, 0)
-                    if side == 0:
-                        arrived = jnp.concatenate([got, back], axis=1)
-                        arrived = jnp.where(row < 4, arrived, 0.0)
-                    else:
-                        arrived = jnp.concatenate([back, got], axis=1)
-                        arrived = jnp.where(row >= 4, arrived, 0.0)
-                    at = 128 * a + 32 * b
-                    arrived = arrived.reshape(32, 128)
-                    for ref, scale in targets:
-                        ref[c, at : at + 32, :] = (
-                            ref[c, at : at + 32, :] + (scale * PENALTY) * arrived
-                        )
-
-    for which, side, _, takes in halos:
-
-        @pl.when(jnp.logical_not(takes))
-        def _():
-            buffer = recv_x if which == 0 else recv_y
-            for stage in range(2 * phases):
-                for c in range(3):
-                    buffer[stage, side, c] = jnp.zeros(buffer.shape[3:], jnp.float32)
+    for axis, buffer in ((0, recv_x), (1, recv_y)):
+        for side in range(2):
+
+            @pl.when(jnp.logical_not(takes[axis][side]))
+            def _():
+                for stage in range(2 * phases):
+                    for part in range(2):
+                        for c in range(3):
+                            buffer[stage, side, part, c] = jnp.zeros(buffer.shape[4:], jnp.float32)
 
     loads[0].wait()
     pack_phase(0)
@@ -353,25 +399,27 @@
                 ]
 
     finish_phase(0)
+    rims(state, 0, -1, 0.0, False, True)
     for s in range(phases):
         stage = 2 * s
-        begin(state, s, stage)
-        if s + 1 < phases:
+        last = s + 1 == phases
+        inner(state, s)
+        if not last:
             send_phase(s + 1)
         for a in range(4):
             b, r = volume(state, a)
             for c in range(3):
                 store(middle, c, a, b[c] + STEP_SIZE * r[c])
-                store(half, c, a, b[c] + (0.5 * STEP_SIZE) * r[c])
-        add_halo(stage, [(middle, STEP_SIZE), (half, 0.5 * STEP_SIZE)])
-        begin(middle, s, stage + 1)
+        rims(middle, s, stage, STEP_SIZE, True, True)
+        inner(middle, s)
         for a in range(4):
-            _, r = volume(middle, a)
+            b, r = volume(middle, a)
             for c in range(3):
-                store(state, c, a, load(half, c, a) + (0.5 * STEP_SIZE) * r[c])
-        if s + 1 < phases:
+                mean = 0.5 * (load(state, c, a) + b[c])
+                store(state, c, a, mean + (0.5 * STEP_SIZE) * r[c])
+        if not last:
             finish_phase(s + 1)
-        add_halo(stage + 1, [(state, 0.5 * STEP_SIZE)])
+        rims(state, s + 1, stage + 1, 0.5 * STEP_SIZE, True, not last)
 
     for k in range(krylov):
         for c in range(3):
@@ -411,21 +459,20 @@
             pltpu.VMEM((comps, lines, depth), f32),
             pltpu.VMEM((comps, lines, depth), f32),
             pltpu.VMEM((comps, lines, depth), f32),
-            pltpu.VMEM((comps, lines, depth), f32),
-            pltpu.VMEM((stages, 2, comps, 128, depth), f32),
-            pltpu.VMEM((stages, 2, comps, 128, depth), f32),
-            pltpu.VMEM((stages, 2, comps, 64, depth), f32),
-            pltpu.VMEM((stages, 2, comps, 64, depth), f32),
+            pltpu.VMEM((stages, 2, 2, comps, 64, depth), f32),
+            pltpu.VMEM((stages, 2, 2, comps, 64, depth), f32),
+            pltpu.VMEM((stages, 2, 2, comps, 32, depth), f32),
+            pltpu.VMEM((stages, 2, 2, comps, 32, depth), f32),
             pltpu.SemaphoreType.DMA((phases, devices)),
             pltpu.SemaphoreType.DMA((phases, devices)),
-            pltpu.SemaphoreType.DMA((stages, 2)),
-            pltpu.SemaphoreType.DMA((stages, 2)),
-            pltpu.SemaphoreType.DMA((stages, 2)),
-            pltpu.SemaphoreType.DMA((stages, 2)),
+            pltpu.SemaphoreType.DMA((stages, 2, 2)),
+            pltpu.SemaphoreType.DMA((stages, 2, 2)),
+            pltpu.SemaphoreType.DMA((stages, 2, 2)),
+            pltpu.SemaphoreType.DMA((stages, 2, 2)),
             pltpu.SemaphoreType.DMA((phases + 1,)),
         ],
         compiler_params=pltpu.CompilerParams(
-            collective_id=0, has_side_effects=True, vmem_limit_bytes=59392 * 1024
+            collective_id=0, has_side_effects=True, vmem_limit_bytes=58048 * 1024
         ),
     )(
         fields.reshape(krylov, comps, rows, depth),

time: 40.8 us -> 38.4 us (0.941)
  Pallas kernels: 38.6 us -> 36 us
    pallas_call x1, Pallas kernels: 38.6 us -> 36 us  [shards(): pl.pallas_call(body, out_shape=jax.ShapeDtypeStruct((krylov, comps, rows,...]
where the time goes in v2:
time: 38.4 us; the launch traced here: 38.1 us
  Pallas kernels  36 us (94%)
  local copies, waits for them, and re-layouts  2.06 us (5%)
    pallas_call x1, Pallas kernels, shards(): pl.pallas_call(body, out_shape=jax.ShapeDtypeStruct((krylov, comps, rows,...  36 us
    unnamed x1, local copies, waits for them, and re-layouts  2.06 us

profile of v2, /device:TPU:3, one launch (start us, length us, event | category | flops | bytes accessed | tf_op | source)
XLA Modules:
  0.0 38.1 jit_solution(15375857941301571450)
XLA Ops:
  0.0 36.0 %shard_map.28 = f32[4,3,128,128]{3,2,1,0:T(8,128)} custom-call(f32[4,3,128,128]{3,2,1,0:T(8,128)} %bitcast.6, f32[2,3,4,8,8,64]{5,4,3,2,1,0:T(8,128)} %bitcast.7), custom_call_target="tpu_custom_call" | custom-call | tf_op jit(solution)/shard_map/pallas_call | solution.py:447
  36.0 2.1 %copy.5 = f32[4,3,64,1,2,128]{5,4,3,2,1,0:T(2,128)} copy(f32[4,3,64,1,2,128]{5,4,3,2,1,0:T(2,128)} %bitcast.5) | data formatting | bytes 1572864

commit v3 on v2

--- a/solution.py
+++ b/solution.py
@@ -80,6 +80,7 @@
     send_v,
     recv_v,
     layers,
+    turned,
     speeds,
     state,
     middle,
@@ -126,15 +127,18 @@
 
     lane8 = lax.broadcasted_iota(jnp.int32, (wide_y, 128), 1)
 
+    def pack_column(s, x):
+        for c in range(3):
+            for z in range(slab):
+                tile = speed_ref[s, c, z, x]
+                wide = jnp.concatenate([tile, tile], axis=1)
+                wide = jnp.where(lane8 < 64, wide, pltpu.roll(wide, wide_y - 1, axis=0))
+                for g in range(count_y):
+                    send_v[s, x * count_y + g, c, z : z + 1, :] = wide[2 * g : 2 * g + 1]
+
     def pack_phase(s):
         def pack(x, carry):
-            for c in range(3):
-                for z in range(slab):
-                    tile = speed_ref[s, c, z, x]
-                    wide = jnp.concatenate([tile, tile], axis=1)
-                    wide = jnp.where(lane8 < 64, wide, pltpu.roll(wide, wide_y - 1, axis=0))
-                    for g in range(count_y):
-                        send_v[s, x * count_y + g, c, z : z + 1, :] = wide[2 * g : 2 * g + 1]
+            pack_column(s, x)
             return carry
 
         lax.fori_loop(0, count_x, pack, 0)
@@ -158,6 +162,8 @@
         lax.fori_loop(1, devices, send, 0)
         pltpu.make_async_copy(send_v.at[s, me], recv_v.at[s, me], sem_vr.at[s, me]).start()
 
+    row2 = lax.broadcasted_iota(jnp.int32, (8, 128), 0)
+
     def finish_phase(s):
         def take(src, carry):
             pltpu.make_async_copy(recv_v.at[s, src], recv_v.at[s, src], sem_vr.at[s, src]).wait()
@@ -167,12 +173,15 @@
         for c in range(3):
             for src in range(devices):
                 layers[c, slab * src : slab * (src + 1), :] = recv_v[s, src, c]
-            turned = layers[c].T
-            for y in range(2):
-                for i in range(8):
-                    rows = turned[64 * y + 8 * i : 64 * y + 8 * (i + 1)]
-                    for k in range(4):
-                        speeds[s, c, pl.ds(64 * i + 4 * y + k, 8, stride=8), :] = rows
+            turned[c] = layers[c].T
+
+    def spread_block(s, a, b):
+        for c in range(3):
+            for i in range(4):
+                node = 16 * a + 4 * b + i
+                first = jnp.broadcast_to(turned[c, node : node + 1, :], (8, 128))
+                second = jnp.broadcast_to(turned[c, 64 + node : 65 + node, :], (8, 128))
+                speeds[c, 8 * node : 8 * (node + 1), :] = jnp.where(row2 < 4, first, second)
 
     def drain_phase(s):
         def drain(i, carry):
@@ -234,10 +243,12 @@
     def block(a, b):
         return slice(128 * a + 32 * b, 128 * a + 32 * (b + 1))
 
-    def cross_block(field, s, a, b):
+    def cross_block(field, fresh, a, b):
+        if fresh is not None:
+            spread_block(fresh, a, b)
         at = block(a, b)
         f = [field[c, at, :].reshape(4, 8, 128) for c in range(3)]
-        u = [speeds[s, c, at, :].reshape(4, 8, 128) for c in range(3)]
+        u = [speeds[c, at, :].reshape(4, 8, 128) for c in range(3)]
         e = [u[1] * f[2] - u[2] * f[1], u[2] * f[0] - u[0] * f[2], u[0] * f[1] - u[1] * f[0]]
         for c in range(3):
             elec[c, at, :] = e[c].reshape(32, 128)
@@ -289,12 +300,20 @@
             found.append(full.reshape(32, 128))
         return found
 
+    def emit_block(a, b):
+        j = 4 * a + b
+        for k in range(krylov):
+            for c in range(3):
+                out_ref[k, c, 8 * j : 8 * (j + 1), :] = state[
+                    c, pl.ds(32 * j + k, 8, stride=4), :
+                ]
+
     def add_block(target, a, b, found, scale):
         at = block(a, b)
         for c in range(3):
             target[c, at, :] = target[c, at, :] + (scale * PENALTY) * found[c]
 
-    def rims(target, s, stage, scale, arrive, onward):
+    def rims(target, fresh, stage, scale, arrive, onward):
         for a in (0, 3):
             if arrive:
                 halo_wait(stage, 0, a // 3, 0)
@@ -302,8 +321,10 @@
                 if arrive:
                     add_block(target, a, b, arrived_x(stage, a, b), scale)
                 if onward:
-                    f, e = cross_block(target, s, a, b)
+                    f, e = cross_block(target, fresh, a, b)
                     pack_x(stage + 1, a, b, f, e)
+                else:
+                    emit_block(a, b)
             if onward:
                 halo_start(stage + 1, 0, 1 - a // 3, 0)
         for b in (0, 3):
@@ -313,8 +334,10 @@
                 if arrive:
                     add_block(target, a, b, arrived_y(stage, a, b), scale)
                 if onward:
-                    f, e = cross_block(target, s, a, b)
+                    f, e = cross_block(target, fresh, a, b)
                     pack_y(stage + 1, a, b, f, e)
+                else:
+                    emit_block(a, b)
             if onward:
                 halo_start(stage + 1, 1, 1 - b // 3, 0)
         if arrive:
@@ -328,19 +351,21 @@
                     fy = arrived_y(stage, a, b)
                     add_block(target, a, b, [fx[c] + fy[c] for c in range(3)], scale)
                 if onward:
-                    f, e = cross_block(target, s, a, b)
+                    f, e = cross_block(target, fresh, a, b)
                     pack_x(stage + 1, a, b, f, e)
                     pack_y(stage + 1, a, b, f, e)
+                else:
+                    emit_block(a, b)
             if onward:
                 halo_start(stage + 1, 0, 1 - a // 3, 1)
         if onward:
             for side in range(2):
                 halo_start(stage + 1, 1, side, 1)
 
-    def inner(field, s):
+    def inner(field, fresh):
         for a in (1, 2):
             for b in (1, 2):
-                cross_block(field, s, a, b)
+                cross_block(field, fresh, a, b)
 
     def volume(field, a):
         b = [load(field, c, a) for c in range(3)]
@@ -410,23 +435,20 @@
             b, r = volume(state, a)
             for c in range(3):
                 store(middle, c, a, b[c] + STEP_SIZE * r[c])
-        rims(middle, s, stage, STEP_SIZE, True, True)
-        inner(middle, s)
+        rims(middle, None, stage, STEP_SIZE, True, True)
+        inner(middle, None)
         for a in range(4):
             b, r = volume(middle, a)
             for c in range(3):
                 mean = 0.5 * (load(state, c, a) + b[c])
                 store(state, c, a, mean + (0.5 * STEP_SIZE) * r[c])
-        if not last:
+        if last:
+            for a in (1, 2):
+                for b in (1, 2):
+                    emit_block(a, b)
+        else:
             finish_phase(s + 1)
         rims(state, s + 1, stage + 1, 0.5 * STEP_SIZE, True, not last)
-
-    for k in range(krylov):
-        for c in range(3):
-            for j in range(16):
-                out_ref[k, c, 8 * j : 8 * (j + 1), :] = state[
-                    c, pl.ds(32 * j + k, 8, stride=4), :
-                ]
 
     for s in range(phases):
         drain_phase(s)
@@ -455,7 +477,8 @@
             pltpu.VMEM((phases, devices, comps, slab, 128), f32),
             pltpu.VMEM((phases, devices, comps, slab, 128), f32),
             pltpu.VMEM((comps, depth, 128), f32),
-            pltpu.VMEM((phases, comps, lines, depth), f32),
+            pltpu.VMEM((comps, 128, depth), f32),
+            pltpu.VMEM((comps, lines, depth), f32),
             pltpu.VMEM((comps, lines, depth), f32),
             pltpu.VMEM((comps, lines, depth), f32),
             pltpu.VMEM((comps, lines, depth), f32),
@@ -472,7 +495,7 @@
             pltpu.SemaphoreType.DMA((phases + 1,)),
         ],
         compiler_params=pltpu.CompilerParams(
-            collective_id=0, has_side_effects=True, vmem_limit_bytes=58048 * 1024
+            collective_id=0, has_side_effects=True, vmem_limit_bytes=55296 * 1024
         ),
     )(
         fields.reshape(krylov, comps, rows, depth),

time: 38.4 us -> 38.3 us (level)
  no operation moved by 1% of the time
where the time goes in v3:
time: 38.3 us; the launch traced here: 38 us
  Pallas kernels  36 us (94%)
  local copies, waits for them, and re-layouts  2.06 us (5%)
    pallas_call x1, Pallas kernels, shards(): pl.pallas_call(body, out_shape=jax.ShapeDtypeStruct((krylov, comps, rows,...  36 us
    unnamed x1, local copies, waits for them, and re-layouts  2.06 us

profile of v3, /device:TPU:3, one launch (start us, length us, event | category | flops | bytes accessed | tf_op | source)
XLA Modules:
  0.0 38.0 jit_solution(2493865943925235390)
XLA Ops:
  0.0 36.0 %shard_map.28 = f32[4,3,128,128]{3,2,1,0:T(8,128)} custom-call(f32[4,3,128,128]{3,2,1,0:T(8,128)} %bitcast.6, f32[2,3,4,8,8,64]{5,4,3,2,1,0:T(8,128)} %bitcast.7), custom_call_target="tpu_custom_call" | custom-call | tf_op jit(solution)/shard_map/pallas_call | solution.py:469
  36.0 2.1 %copy.5 = f32[4,3,64,1,2,128]{5,4,3,2,1,0:T(2,128)} copy(f32[4,3,64,1,2,128]{5,4,3,2,1,0:T(2,128)} %bitcast.5) | data formatting | bytes 1572864

commit v4 on v3

--- a/solution.py
+++ b/solution.py
@@ -96,6 +96,12 @@
     sem_ys,
     sem_yr,
     sem_in,
+    ghost_x,
+    ghost_y,
+    sem_gxs,
+    sem_gxr,
+    sem_gys,
+    sem_gyr,
 ):
     gx = lax.axis_index("gx")
     gy = lax.axis_index("gy")
@@ -173,14 +179,15 @@
         for c in range(3):
             for src in range(devices):
                 layers[c, slab * src : slab * (src + 1), :] = recv_v[s, src, c]
-            turned[c] = layers[c].T
+            turned[s, c] = layers[c].T.reshape(2, 4, 16, 128)
 
     def spread_block(s, a, b):
         for c in range(3):
             for i in range(4):
                 node = 16 * a + 4 * b + i
-                first = jnp.broadcast_to(turned[c, node : node + 1, :], (8, 128))
-                second = jnp.broadcast_to(turned[c, 64 + node : 65 + node, :], (8, 128))
+                at = 4 * b + i
+                first = jnp.broadcast_to(turned[s, c, 0, a, at : at + 1, :], (8, 128))
+                second = jnp.broadcast_to(turned[s, c, 1, a, at : at + 1, :], (8, 128))
                 speeds[c, 8 * node : 8 * (node + 1), :] = jnp.where(row2 < 4, first, second)
 
     def drain_phase(s):
@@ -213,6 +220,47 @@
             device_id_type=MESH,
         )
 
+    def ghost_copy(axis, side):
+        step = 1 if side == 0 else -1
+        if axis == 0:
+            return pltpu.make_async_remote_copy(
+                src_ref=turned.at[0, :, :, 3 - 3 * side],
+                dst_ref=ghost_x.at[side],
+                send_sem=sem_gxs.at[side],
+                recv_sem=sem_gxr.at[side],
+                device_id=(gx + step, gy),
+                device_id_type=MESH,
+            )
+        return pltpu.make_async_remote_copy(
+            src_ref=turned.at[0, :, 1 - side, :, pl.ds(8 - 8 * side, 8)],
+            dst_ref=ghost_y.at[side],
+            send_sem=sem_gys.at[side],
+            recv_sem=sem_gyr.at[side],
+            device_id=(gx, gy + step),
+            device_id_type=MESH,
+        )
+
+    def ghost_start():
+        for axis in range(2):
+            for side in range(2):
+
+                @pl.when(sends[axis][side])
+                def _():
+                    ghost_copy(axis, side).start()
+
+    def ghost_wait(axis, side):
+        @pl.when(takes[axis][side])
+        def _():
+            ghost_copy(axis, side).wait_recv()
+
+    def ghost_drain():
+        for axis in range(2):
+            for side in range(2):
+
+                @pl.when(sends[axis][side])
+                def _():
+                    ghost_copy(axis, side).wait_send()
+
     sends = [[has_high_x, has_low_x], [has_high_y, has_low_y]]
     takes = [[has_low_x, has_high_x], [has_low_y, has_high_y]]
 
@@ -249,27 +297,32 @@
         at = block(a, b)
         f = [field[c, at, :].reshape(4, 8, 128) for c in range(3)]
         u = [speeds[c, at, :].reshape(4, 8, 128) for c in range(3)]
-        e = [u[1] * f[2] - u[2] * f[1], u[2] * f[0] - u[0] * f[2], u[0] * f[1] - u[1] * f[0]]
+        e = cross(u, f)
         for c in range(3):
             elec[c, at, :] = e[c].reshape(32, 128)
         return f, e
 
-    def pack_x(stage, a, b, f, e):
+    def cross(u, f):
+        return [u[1] * f[2] - u[2] * f[1], u[2] * f[0] - u[0] * f[2], u[0] * f[1] - u[1] * f[0]]
+
+    def face_x(a, f, e):
         if a == 0:
-            face = [f[0], f[1] - e[2], f[2] + e[1]]
-        else:
-            face = [f[0], f[1] + e[2], f[2] - e[1]]
+            return [f[0], f[1] - e[2], f[2] + e[1]]
+        return [f[0], f[1] + e[2], f[2] - e[1]]
+
+    def face_y(b, f, e):
+        if b == 0:
+            return [f[0] + e[2], f[1], f[2] - e[0]]
+        return [f[0] - e[2], f[1], f[2] + e[0]]
+
+    def pack_x(stage, a, b, face):
         part, slot = (0, b - 1) if b in (1, 2) else (1, b // 3)
         for c in range(3):
             send_x[stage, 1 - a // 3, part, c, 32 * slot : 32 * (slot + 1), :] = face[c].reshape(
                 32, 128
             )
 
-    def pack_y(stage, a, b, f, e):
-        if b == 0:
-            face = [f[0] + e[2], f[1], f[2] - e[0]]
-        else:
-            face = [f[0] - e[2], f[1], f[2] + e[0]]
+    def pack_y(stage, a, b, face):
         part, slot = (0, a - 1) if a in (1, 2) else (1, a // 3)
         for c in range(3):
             if b == 0:
@@ -282,23 +335,45 @@
 
     def arrived_x(stage, a, b):
         part, slot = (0, b - 1) if b in (1, 2) else (1, b // 3)
-        return [
-            recv_x[stage, a // 3, part, c, 32 * slot : 32 * (slot + 1), :] for c in range(3)
-        ]
+        side = a // 3
+        f = [recv_x[stage, side, part, c, 32 * slot : 32 * (slot + 1), :] for c in range(3)]
+        if stage > 0:
+            return f
+        f = [item.reshape(4, 8, 128) for item in f]
+        u = []
+        for c in range(3):
+            nodes = []
+            for i in range(4 * b, 4 * b + 4):
+                first = jnp.broadcast_to(ghost_x[side, c, 0, i : i + 1, :], (8, 128))
+                second = jnp.broadcast_to(ghost_x[side, c, 1, i : i + 1, :], (8, 128))
+                nodes.append(jnp.where(row2 < 4, first, second))
+            u.append(jnp.stack(nodes))
+        return [item.reshape(32, 128) for item in face_x(3 - a, f, cross(u, f))]
 
     def arrived_y(stage, a, b):
         part, slot = (0, a - 1) if a in (1, 2) else (1, a // 3)
-        found = []
-        for c in range(3):
-            got = recv_y[stage, b // 3, part, c, 16 * slot : 16 * (slot + 1), :]
+        side = b // 3
+        f = []
+        for c in range(3):
+            got = recv_y[stage, side, part, c, 16 * slot : 16 * (slot + 1), :]
             got = got.reshape(2, 8, 128)
             back = turn(got, 4, 0)
             if b == 0:
                 full = jnp.where(row3 < 4, jnp.concatenate([got, back], axis=0), 0.0)
             else:
                 full = jnp.where(row3 >= 4, jnp.concatenate([back, got], axis=0), 0.0)
-            found.append(full.reshape(32, 128))
-        return found
+            f.append(full)
+        if stage == 0:
+            u = []
+            for c in range(3):
+                low = 4 - 4 * side
+                nodes = [
+                    jnp.broadcast_to(ghost_y[side, c, a, i : i + 1, :], (8, 128))
+                    for i in range(low, low + 4)
+                ]
+                u.append(jnp.stack(nodes))
+            f = face_y(3 - b, f, cross(u, f))
+        return [item.reshape(32, 128) for item in f]
 
     def emit_block(a, b):
         j = 4 * a + b
@@ -313,47 +388,45 @@
         for c in range(3):
             target[c, at, :] = target[c, at, :] + (scale * PENALTY) * found[c]
 
-    def rims(target, fresh, stage, scale, arrive, onward):
+    def rims(target, fresh, stage, scale, onward):
         for a in (0, 3):
-            if arrive:
-                halo_wait(stage, 0, a // 3, 0)
+            halo_wait(stage, 0, a // 3, 0)
+            if stage == 0:
+                ghost_wait(0, a // 3)
             for b in (1, 2):
-                if arrive:
-                    add_block(target, a, b, arrived_x(stage, a, b), scale)
+                add_block(target, a, b, arrived_x(stage, a, b), scale)
                 if onward:
                     f, e = cross_block(target, fresh, a, b)
-                    pack_x(stage + 1, a, b, f, e)
+                    pack_x(stage + 1, a, b, face_x(a, f, e))
                 else:
                     emit_block(a, b)
             if onward:
                 halo_start(stage + 1, 0, 1 - a // 3, 0)
         for b in (0, 3):
-            if arrive:
-                halo_wait(stage, 1, b // 3, 0)
+            halo_wait(stage, 1, b // 3, 0)
+            if stage == 0:
+                ghost_wait(1, b // 3)
             for a in (1, 2):
-                if arrive:
-                    add_block(target, a, b, arrived_y(stage, a, b), scale)
+                add_block(target, a, b, arrived_y(stage, a, b), scale)
                 if onward:
                     f, e = cross_block(target, fresh, a, b)
-                    pack_y(stage + 1, a, b, f, e)
+                    pack_y(stage + 1, a, b, face_y(b, f, e))
                 else:
                     emit_block(a, b)
             if onward:
                 halo_start(stage + 1, 1, 1 - b // 3, 0)
-        if arrive:
-            for axis in range(2):
-                for side in range(2):
-                    halo_wait(stage, axis, side, 1)
+        for axis in range(2):
+            for side in range(2):
+                halo_wait(stage, axis, side, 1)
         for a in (0, 3):
             for b in (0, 3):
-                if arrive:
-                    fx = arrived_x(stage, a, b)
-                    fy = arrived_y(stage, a, b)
-                    add_block(target, a, b, [fx[c] + fy[c] for c in range(3)], scale)
+                fx = arrived_x(stage, a, b)
+                fy = arrived_y(stage, a, b)
+                add_block(target, a, b, [fx[c] + fy[c] for c in range(3)], scale)
                 if onward:
                     f, e = cross_block(target, fresh, a, b)
-                    pack_x(stage + 1, a, b, f, e)
-                    pack_y(stage + 1, a, b, f, e)
+                    pack_x(stage + 1, a, b, face_x(a, f, e))
+                    pack_y(stage + 1, a, b, face_y(b, f, e))
                 else:
                     emit_block(a, b)
             if onward:
@@ -361,6 +434,19 @@
         if onward:
             for side in range(2):
                 halo_start(stage + 1, 1, side, 1)
+
+    def first_faces():
+        for a in range(4):
+            for b in range(4):
+                f = [state[c, block(a, b), :].reshape(4, 8, 128) for c in range(3)]
+                if a in (0, 3):
+                    pack_x(0, a, b, f)
+                if b in (0, 3):
+                    pack_y(0, a, b, f)
+        for axis in range(2):
+            for side in range(2):
+                for part in range(2):
+                    halo_start(0, axis, side, part)
 
     def inner(field, fresh):
         for a in (1, 2):
@@ -397,6 +483,13 @@
             r[c] = r[c] + PENALTY * jump
         return b, r
 
+    for axis, buffer in ((0, ghost_x), (1, ghost_y)):
+        for side in range(2):
+
+            @pl.when(jnp.logical_not(takes[axis][side]))
+            def _():
+                buffer[side] = jnp.zeros(buffer.shape[1:], jnp.float32)
+
     for axis, buffer in ((0, recv_x), (1, recv_y)):
         for side in range(2):
 
@@ -411,9 +504,6 @@
     pack_phase(0)
     pl.semaphore_wait(barrier, devices - 1)
     send_phase(0)
-    for s in range(1, phases):
-        loads[s].wait()
-        pack_phase(s)
     loads[phases].wait()
 
     for k in range(krylov):
@@ -422,12 +512,23 @@
                 state[c, pl.ds(32 * j + k, 8, stride=4), :] = fields_ref[
                     k, c, 8 * j : 8 * (j + 1), :
                 ]
+    first_faces()
+    for s in range(1, phases):
+        loads[s].wait()
+        pack_phase(s)
 
     finish_phase(0)
-    rims(state, 0, -1, 0.0, False, True)
+    ghost_start()
     for s in range(phases):
         stage = 2 * s
         last = s + 1 == phases
+        if s == 0:
+            for a in (0, 3):
+                for b in range(4):
+                    cross_block(state, 0, a, b)
+            for a in (1, 2):
+                for b in (0, 3):
+                    cross_block(state, 0, a, b)
         inner(state, s)
         if not last:
             send_phase(s + 1)
@@ -435,7 +536,7 @@
             b, r = volume(state, a)
             for c in range(3):
                 store(middle, c, a, b[c] + STEP_SIZE * r[c])
-        rims(middle, None, stage, STEP_SIZE, True, True)
+        rims(middle, None, stage, STEP_SIZE, True)
         inner(middle, None)
         for a in range(4):
             b, r = volume(middle, a)
@@ -448,10 +549,11 @@
                     emit_block(a, b)
         else:
             finish_phase(s + 1)
-        rims(state, s + 1, stage + 1, 0.5 * STEP_SIZE, True, not last)
+        rims(state, s + 1, stage + 1, 0.5 * STEP_SIZE, not last)
 
     for s in range(phases):
         drain_phase(s)
+    ghost_drain()
     for stage in range(2 * phases):
         halo_drain(stage)
 
@@ -477,7 +579,7 @@
             pltpu.VMEM((phases, devices, comps, slab, 128), f32),
             pltpu.VMEM((phases, devices, comps, slab, 128), f32),
             pltpu.VMEM((comps, depth, 128), f32),
-            pltpu.VMEM((comps, 128, depth), f32),
+            pltpu.VMEM((phases, comps, 2, 4, 16, depth), f32),
             pltpu.VMEM((comps, lines, depth), f32),
             pltpu.VMEM((comps, lines, depth), f32),
             pltpu.VMEM((comps, lines, depth), f32),
@@ -493,9 +595,15 @@
             pltpu.SemaphoreType.DMA((stages, 2, 2)),
             pltpu.SemaphoreType.DMA((stages, 2, 2)),
             pltpu.SemaphoreType.DMA((phases + 1,)),
+            pltpu.VMEM((2, comps, 2, 16, depth), f32),
+            pltpu.VMEM((2, comps, 4, 8, depth), f32),
+            pltpu.SemaphoreType.DMA((2,)),
+            pltpu.SemaphoreType.DMA((2,)),
+            pltpu.SemaphoreType.DMA((2,)),
+            pltpu.SemaphoreType.DMA((2,)),
         ],
         compiler_params=pltpu.CompilerParams(
-            collective_id=0, has_side_effects=True, vmem_limit_bytes=55296 * 1024
+            collective_id=0, has_side_effects=True, vmem_limit_bytes=53248 * 1024
         ),
     )(
         fields.reshape(krylov, comps, rows, depth),

time: 38.3 us -> 35.6 us (0.930)
  Pallas kernels: 36 us -> 33.4 us
    pallas_call x1, Pallas kernels: 36 us -> 33.4 us  [shards(): pl.pallas_call(body, out_shape=jax.ShapeDtypeStruct((krylov, comps, rows,...]
    unnamed x1 -> x3, local copies, waits for them, and re-layouts: 2.06 us -> 2.01 us
where the time goes in v4:
time: 35.6 us; the launch traced here: 35.5 us
  Pallas kernels  33.4 us (94%)
  local copies, waits for them, and re-layouts  2.01 us (6%)
    pallas_call x1, Pallas kernels, shards(): pl.pallas_call(body, out_shape=jax.ShapeDtypeStruct((krylov, comps, rows,...  33.4 us
    unnamed x3, local copies, waits for them, and re-layouts  2.01 us

profile of v4, /device:TPU:3, one launch (start us, length us, event | category | flops | bytes accessed | tf_op | source)
XLA Modules:
  0.0 35.5 jit_solution(16536146377384495110)
XLA Ops:
  0.0 0.0 copy-start
  0.0 1.1 %copy-done = f32[4,3,64,1,2,128]{5,4,3,2,1,0:T(2,128)S(1)} copy-done((f32[4,3,64,1,2,128]{5,4,3,2,1,0:T(2,128)S(1)}, f32[4,3,64,1,2,128]{5,4,3,2,1,0:T(2,128)}, u32[]{:S(2)}) %copy-start) | copy-done | bytes 786456
  1.1 33.4 %shard_map.28 = f32[4,3,128,128]{3,2,1,0:T(8,128)S(1)} custom-call(f32[4,3,128,128]{3,2,1,0:T(8,128)S(1)} %bitcast.6, f32[2,3,4,8,8,64]{5,4,3,2,1,0:T(8,128)} %bitcast.7), custom_call_target="tpu_custom_call" | custom-call | tf_op jit(solution)/shard_map/pallas_call | solution.py:571
  34.6 0.9 %copy.5 = f32[4,3,64,1,2,128]{5,4,3,2,1,0:T(2,128)} copy(f32[4,3,64,1,2,128]{5,4,3,2,1,0:T(2,128)S(1)} %bitcast.5) | data formatting | bytes 1572864
Async XLA Ops:
  0.0 1.1 %copy-start = (f32[4,3,64,1,2,128]{5,4,3,2,1,0:T(2,128)S(1)}, f32[4,3,64,1,2,128]{5,4,3,2,1,0:T(2,128)}, u32[]{:S(2)}) copy-start(f32[4,3,64,1,2,128]{5,4,3,2,1,0:T(2,128)} %param.2) | copy-start | bytes 2359300

commit v5 on v4

--- a/solution.py
+++ b/solution.py
@@ -516,6 +516,7 @@
     for s in range(1, phases):
         loads[s].wait()
         pack_phase(s)
+        send_phase(s)
 
     finish_phase(0)
     ghost_start()
@@ -530,8 +531,6 @@
                 for b in (0, 3):
                     cross_block(state, 0, a, b)
         inner(state, s)
-        if not last:
-            send_phase(s + 1)
         for a in range(4):
             b, r = volume(state, a)
             for c in range(3):
@@ -603,7 +602,7 @@
             pltpu.SemaphoreType.DMA((2,)),
         ],
         compiler_params=pltpu.CompilerParams(
-            collective_id=0, has_side_effects=True, vmem_limit_bytes=53248 * 1024
+            collective_id=0, has_side_effects=True, vmem_limit_bytes=54016 * 1024
         ),
     )(
         fields.reshape(krylov, comps, rows, depth),

time: 35.6 us -> 34.3 us (0.963)
  local copies, waits for them, and re-layouts: 2.01 us -> 0.88 us
    unnamed x3 -> x1, local copies, waits for them, and re-layouts: 2.01 us -> 0.88 us
where the time goes in v5:
time: 34.3 us; the launch traced here: 34.1 us
  Pallas kernels  33.2 us (97%)
  local copies, waits for them, and re-layouts  0.88 us (3%)
    pallas_call x1, Pallas kernels, shards(): pl.pallas_call(body, out_shape=jax.ShapeDtypeStruct((krylov, comps, rows,...  33.2 us
    unnamed x1, local copies, waits for them, and re-layouts  0.88 us

profile of v5, /device:TPU:3, one launch (start us, length us, event | category | flops | bytes accessed | tf_op | source)
XLA Modules:
  0.0 34.1 jit_solution(18012038481827716428)
XLA Ops:
  0.0 33.2 %shard_map.28 = f32[4,3,128,128]{3,2,1,0:T(8,128)S(1)} custom-call(f32[4,3,128,128]{3,2,1,0:T(8,128)} %bitcast.6, f32[2,3,4,8,8,64]{5,4,3,2,1,0:T(8,128)} %bitcast.7), custom_call_target="tpu_custom_call" | custom-call | tf_op jit(solution)/shard_map/pallas_call | solution.py:570
  33.2 0.9 %copy.5 = f32[4,3,64,1,2,128]{5,4,3,2,1,0:T(2,128)} copy(f32[4,3,64,1,2,128]{5,4,3,2,1,0:T(2,128)S(1)} %bitcast.5) | data formatting | bytes 1572864

commit v6 on v5

--- a/solution.py
+++ b/solution.py
@@ -171,14 +171,11 @@
     row2 = lax.broadcasted_iota(jnp.int32, (8, 128), 0)
 
     def finish_phase(s):
-        def take(src, carry):
+        for src in range(devices):
             pltpu.make_async_copy(recv_v.at[s, src], recv_v.at[s, src], sem_vr.at[s, src]).wait()
-            return carry
-
-        lax.fori_loop(0, devices, take, 0)
-        for c in range(3):
-            for src in range(devices):
+            for c in range(3):
                 layers[c, slab * src : slab * (src + 1), :] = recv_v[s, src, c]
+        for c in range(3):
             turned[s, c] = layers[c].T.reshape(2, 4, 16, 128)
 
     def spread_block(s, a, b):
@@ -389,6 +386,19 @@
             target[c, at, :] = target[c, at, :] + (scale * PENALTY) * found[c]
 
     def rims(target, fresh, stage, scale, onward):
+        for b in (0, 3):
+            halo_wait(stage, 1, b // 3, 0)
+            if stage == 0:
+                ghost_wait(1, b // 3)
+            for a in (1, 2):
+                add_block(target, a, b, arrived_y(stage, a, b), scale)
+                if onward:
+                    f, e = cross_block(target, fresh, a, b)
+                    pack_y(stage + 1, a, b, face_y(b, f, e))
+                else:
+                    emit_block(a, b)
+            if onward:
+                halo_start(stage + 1, 1, 1 - b // 3, 0)
         for a in (0, 3):
             halo_wait(stage, 0, a // 3, 0)
             if stage == 0:
@@ -402,19 +412,6 @@
                     emit_block(a, b)
             if onward:
                 halo_start(stage + 1, 0, 1 - a // 3, 0)
-        for b in (0, 3):
-            halo_wait(stage, 1, b // 3, 0)
-            if stage == 0:
-                ghost_wait(1, b // 3)
-            for a in (1, 2):
-                add_block(target, a, b, arrived_y(stage, a, b), scale)
-                if onward:
-                    f, e = cross_block(target, fresh, a, b)
-                    pack_y(stage + 1, a, b, face_y(b, f, e))
-                else:
-                    emit_block(a, b)
-            if onward:
-                halo_start(stage + 1, 1, 1 - b // 3, 0)
         for axis in range(2):
             for side in range(2):
                 halo_wait(stage, axis, side, 1)

time: 34.3 us -> 35.8 us (1.044)
  the two profiles are of different devices: /device:TPU:3 before, /device:TPU:11 now
where the time goes in v6:
time: 35.8 us; the launch traced here: 35.7 us
  Pallas kernels  34.8 us (97%)
  local copies, waits for them, and re-layouts  0.88 us (2%)
    pallas_call x1, Pallas kernels, shards(): pl.pallas_call(body, out_shape=jax.ShapeDtypeStruct((krylov, comps, rows,...  34.8 us
    unnamed x1, local copies, waits for them, and re-layouts  0.88 us

profile of v6, /device:TPU:11, one launch (start us, length us, event | category | flops | bytes accessed | tf_op | source)
XLA Modules:
  0.0 35.7 jit_solution(7453161885707737775)
XLA Ops:
  0.0 34.8 %shard_map.28 = f32[4,3,128,128]{3,2,1,0:T(8,128)S(1)} custom-call(f32[4,3,128,128]{3,2,1,0:T(8,128)} %bitcast.6, f32[2,3,4,8,8,64]{5,4,3,2,1,0:T(8,128)} %bitcast.7), custom_call_target="tpu_custom_call" | custom-call | tf_op jit(solution)/shard_map/pallas_call | solution.py:567
  34.8 0.9 %copy.5 = f32[4,3,64,1,2,128]{5,4,3,2,1,0:T(2,128)} copy(f32[4,3,64,1,2,128]{5,4,3,2,1,0:T(2,128)S(1)} %bitcast.5) | data formatting | bytes 1572864

commit v7 on v5

--- a/solution.py
+++ b/solution.py
@@ -402,19 +402,9 @@
                     emit_block(a, b)
             if onward:
                 halo_start(stage + 1, 0, 1 - a // 3, 0)
-        for b in (0, 3):
-            halo_wait(stage, 1, b // 3, 0)
-            if stage == 0:
-                ghost_wait(1, b // 3)
-            for a in (1, 2):
-                add_block(target, a, b, arrived_y(stage, a, b), scale)
-                if onward:
-                    f, e = cross_block(target, fresh, a, b)
-                    pack_y(stage + 1, a, b, face_y(b, f, e))
-                else:
-                    emit_block(a, b)
-            if onward:
-                halo_start(stage + 1, 1, 1 - b // 3, 0)
+        if stage == 0:
+            for side in range(2):
+                ghost_wait(1, side)
         for axis in range(2):
             for side in range(2):
                 halo_wait(stage, axis, side, 1)
@@ -434,6 +424,17 @@
         if onward:
             for side in range(2):
                 halo_start(stage + 1, 1, side, 1)
+        for b in (0, 3):
+            halo_wait(stage, 1, b // 3, 0)
+            for a in (1, 2):
+                add_block(target, a, b, arrived_y(stage, a, b), scale)
+                if onward:
+                    f, e = cross_block(target, fresh, a, b)
+                    pack_y(stage + 1, a, b, face_y(b, f, e))
+                else:
+                    emit_block(a, b)
+            if onward:
+                halo_start(stage + 1, 1, 1 - b // 3, 0)
 
     def first_faces():
         for a in range(4):

time: 34.3 us -> 34.9 us (1.017)
  the two profiles are of different devices: /device:TPU:3 before, /device:TPU:0 now
where the time goes in v7:
time: 34.9 us; the launch traced here: 34.7 us
  Pallas kernels  33.9 us (97%)
  local copies, waits for them, and re-layouts  0.88 us (3%)
    pallas_call x1, Pallas kernels, shards(): pl.pallas_call(body, out_shape=jax.ShapeDtypeStruct((krylov, comps, rows,...  33.9 us
    unnamed x1, local copies, waits for them, and re-layouts  0.88 us

profile of v7, /device:TPU:0, one launch (start us, length us, event | category | flops | bytes accessed | tf_op | source)
XLA Modules:
  0.0 34.7 jit_solution(2285802663294979168)
XLA Ops:
  0.0 33.9 %shard_map.28 = f32[4,3,128,128]{3,2,1,0:T(8,128)S(1)} custom-call(f32[4,3,128,128]{3,2,1,0:T(8,128)} %bitcast.6, f32[2,3,4,8,8,64]{5,4,3,2,1,0:T(8,128)} %bitcast.7), custom_call_target="tpu_custom_call" | custom-call | tf_op jit(solution)/shard_map/pallas_call | solution.py:571
  33.9 0.9 %copy.5 = f32[4,3,64,1,2,128]{5,4,3,2,1,0:T(2,128)} copy(f32[4,3,64,1,2,128]{5,4,3,2,1,0:T(2,128)S(1)} %bitcast.5) | data formatting | bytes 1572864
